TPU v7x, 128 devices: a whole 4x4x4 slice. The times are simulated.
128 devices in a mesh: expert: 16 (over z, x), row: 8 (over y, core).
Axes of the slice: x: 4, y: 4, z: 4, core: 2. Of those that a mesh axis runs over, the one named last changes fastest.
Arguments:
- base_weights: bfloat16 [32, 2, 1536, 4096], P(None, None, 'row', 'expert'), may hold values from -6 to 6
- adapter_up_factor: bfloat16 [32, 2, 64, 1536], P(None, None, None, 'row'), may hold values from -6 to 6
- adapter_down: bfloat16 [32, 2, 64, 4096], P(None, None, 'row', 'expert'), may hold values from -6 to 6
- file_sizes: int32 [16], replicated, may hold values from 1 to 8, 64 in all
- file_writer: int32 [16], replicated, may hold values from 0 to 15, each once
Outputs:
- merged_store: bfloat16 [128, 1536, 4096], P('expert', 'row')
Inputs may be any that keep to these rules, and one draw needn't show every extreme that they name: `file_sizes`: every file holds at least one tensor, together 2 * 32; the largest file holds exactly 8. `file_writer`: each rank along the expert axis owns exactly one file.
All inputs are finite; a program needn't handle non-finite values.
Results may differ from a plain program's by a relative error of at most 0.001.
Values may be sent and summed in bfloat16 or wider, within the bound.
No kernel may reach another device: no remote copies, remote signals or barrier semaphores. Data moves between devices by JAX's collectives and lax.ppermute only.
A program may use at most 192 MiB of HBM per device.

v0:
```python
import jax
import jax.numpy as jnp
from jax import lax
from jax.sharding import PartitionSpec as P

CAP = 8


scaling = 0.125


def slot_lookup_table(file_sizes, file_writer, writers_count):
    writers = jnp.arange(writers_count, dtype=jnp.int32)
    matches = file_writer[None, :] == writers[:, None]
    starts = jnp.cumsum(file_sizes) - file_sizes
    slot_count = jnp.sum(jnp.where(matches, file_sizes[None, :], 0), axis=1)
    slot_first = jnp.sum(jnp.where(matches, starts[None, :], 0), axis=1)
    positions = jnp.arange(CAP, dtype=jnp.int32)
    slot_live = positions[None, :] < slot_count[:, None]
    slot_source = jnp.where(slot_live, slot_first[:, None] + positions[None, :], 0)
    return (slot_source, slot_live)


def body(base_weights, adapter_up_factor, adapter_down, file_sizes, file_writer):
    writers_count = lax.axis_size("expert")
    tensors = base_weights.shape[0] * base_weights.shape[1]
    rows_here = base_weights.shape[2]
    cols_here = base_weights.shape[3]
    rank_full = adapter_up_factor.shape[2]
    slot_source, slot_live = slot_lookup_table(file_sizes, file_writer, writers_count)
    flat_base = base_weights.reshape(tensors, rows_here, cols_here)
    flattened_up = adapter_up_factor.reshape(tensors, rank_full, rows_here)
    active_slot_mask = slot_live[:, :, None, None]
    nothing = jnp.zeros((), jnp.bfloat16)
    factor_pairs = lax.all_gather(adapter_down, "row", axis=2, tiled=True)
    flattened_down = factor_pairs.reshape(tensors, rank_full, cols_here)
    merge_update = jnp.einsum(
        "nlw,nly->nwy", flattened_up, flattened_down, preferred_element_type=jnp.float32
    )
    merged = (flat_base.astype(jnp.float32) + scaling * merge_update).astype(jnp.bfloat16)
    outgoing = jnp.where(active_slot_mask, merged[slot_source], nothing)
    arrived = lax.all_to_all(outgoing, "expert", split_axis=0, concat_axis=3, tiled=True)
    return arrived[0]


def solution(mesh):
    in_specs = (
        P(None, None, "row", "expert"),
        P(None, None, None, "row"),
        P(None, None, "row", "expert"),
        P(),
        P(),
    )
    out_specs = P("expert", "row", None)
    return jax.shard_map(body, mesh=mesh, in_specs=in_specs, out_specs=out_specs, check_vma=False)
```

profile of v0, /device:TPU:0, one launch (start us, length us, event | category | flops | bytes accessed | tf_op | source)
XLA Modules:
  0.0 263.1 jit_solution(14535831901214609025)
XLA Ops:
  6.5 0.0 copy-start
  6.5 0.0 all-gather.2.cloned.1.call-start
  6.5 0.7 all-gather.2.cloned.1.call-update
  7.3 0.7 copy.10
  8.0 0.1 reduce
  8.1 0.7 sub.3
  8.8 0.8 select_reduce_fusion.1
  9.6 0.1 compare_select_fusion
  9.7 0.1 reshape.139
  9.8 0.1 iota_compare_fusion.2
  9.9 28.9 %all-gather.2.cloned.1.call-done = bf16[32,2,64,256]{3,2,1,0:T(8,128)(2,1)} async-done(((bf16[32,2,8,256]{3,2,1,0:T(8,128)(2,1)}), bf16[32,2,64,256]{3,2,1,0:T(8,128)(2,1)}) %all-gather.2.cloned.1.call-update) | async-done | bytes 2097168 | tf_op jit(solution)/shard_map/all_gather | solution.py:35
  38.8 0.0 copy-done
  38.8 8.2 %fusion = bf16[64,192,256]{2,1,0:T(8,128)(2,1)} fusion(bf16[32,2,192,256]{3,2,1,0:T(8,128)(2,1)} %param.5, bf16[64,64,192]{2,1,0:T(8,128)(2,1)S(1)} %bitcast.16, bf16[64,64,256]{2,1,0:T(8,128)(2,1)} %bitcast.19), kind=kOutput, calls=%fused_computation.2 | convolution fusion | flops 415236096 | bytes 16252928 | tf_op jit(solution)/shard_map/nlw,nly->nwy/dot_general | solution.py:37
  47.0 11.3 %gather_fusion = bf16[128,192,256]{2,1,0:T(8,128)(2,1)} fusion(bf16[64,192,256]{2,1,0:T(8,128)(2,1)} %fusion, s32[1024]{0:T(1024)S(1)} %pad_clamp_fusion), kind=kCustom, calls=%fused_computation | custom fusion | bytes 25166336 | tf_op jit(solution)/shard_map/gather | solution.py:41
  58.3 6.4 %broadcast_select_fusion = bf16[16,8,192,256]{3,2,1,0:T(8,128)(2,1)S(1)} fusion(bf16[16,8,192,256]{3,2,1,0:T(8,128)(2,1)} %bitcast.17, pred[16,8]{1,0:T(8,128)(4,1)S(1)} %iota_compare_fusion.2), kind=kLoop, calls=%fused_computation.3 | loop fusion | flops 6291456 | bytes 25165952 | tf_op jit(solution)/shard_map/jit(_where)/select_n | solution.py:41
  64.7 147.9 %all_to_all.15 = bf16[16,8,192,256]{3,2,1,0:T(8,128)(2,1)S(1)} all-to-all(bf16[16,8,192,256]{3,2,1,0:T(8,128)(2,1)S(1)} %broadcast_select_fusion), channel_id=1, replica_groups=mesh['expert'=16,'row'=8] {'expert'}, dimensions={0} | all-to-all | bytes 25165824 | tf_op jit(solution)/shard_map/all_to_all | solution.py:42
  212.6 0.0 copy-start.1
  212.6 24.1 %copy.11 = bf16[1,8,192,16,256]{4,3,2,1,0:T(8,128)(2,1)} copy(bf16[1,8,192,16,256]{4,2,1,3,0:T(8,128)(2,1)S(1)} %bitcast.18) | data formatting | bytes 25165824 | tf_op jit(solution)/shard_map/all_to_all | solution.py:42
  236.7 19.5 %squeeze.3 = bf16[8,192,4096]{2,1,0:T(8,128)(2,1)} reshape(bf16[1,8,192,16,256]{4,3,2,1,0:T(8,128)(2,1)} %copy.11) | data formatting | bytes 25165824 | tf_op jit(solution)/shard_map/squeeze | solution.py:43
  256.2 0.0 copy-done.1
  (2 shorter events, 0.0 us)
Async XLA Ops:
  6.5 32.3 %copy-start = (bf16[32,2,64,192]{3,2,1,0:T(8,128)(2,1)S(1)}, bf16[32,2,64,192]{3,2,1,0:T(8,128)(2,1)}, u32[]{:S(2)}) copy-start(bf16[32,2,64,192]{3,2,1,0:T(8,128)(2,1)} %param.6) | copy-start | bytes 4718596
  6.5 32.3 %all-gather.2.cloned.1.call-start = ((), (), s32[]{:S(2)}) async-start(), calls=%async_computation.1 | async-start | bytes 2359296 | tf_op jit(solution)/shard_map/all_gather | solution.py:35
  212.6 43.6 %copy-start.1 = (bf16[32,2,64,192]{3,2,1,0:T(8,128)(2,1)S(1)}, bf16[32,2,64,192]{3,2,1,0:T(8,128)(2,1)}, u32[]{:S(2)}) copy-start(bf16[32,2,64,192]{3,2,1,0:T(8,128)(2,1)} %param.6) | copy-start | bytes 4718596
Sparse Core Ops, SparseCore 0:
  9.0 29.7 all-gather.1
where the time goes:
time: 264 us; the launch traced here: 263 us
  blocking collectives  148 us (56%)
  local copies, waits for them, and re-layouts  55.7 us (21%)
  waiting for transfers between devices  29.7 us (11%)
  between operations  13.4 us (5%)
  matrix products  8.23 us (3%)
  other arithmetic  8.14 us (3%)
    all_to_all x1, blocking collectives, body(): lax.all_to_all(outgoing, 'expert', split_axis=0, concat_axis=3, tiled=True)  148 us
    all_gather x1, waiting for transfers between devices, body(): factor_pairs = lax.all_gather(adapter_down, 'row', axis=2, tiled=True)  28.9 us
    all_to_all x1, local copies, waits for them, and re-layouts, body(): lax.all_to_all(outgoing, 'expert', split_axis=0, concat_axis=3, tiled=True)  24.1 us
    squeeze x1, local copies, waits for them, and re-layouts, body(): return arrived[0]  19.5 us
    gather x1, local copies, waits for them, and re-layouts, body(): outgoing = jnp.where(active_slot_mask, merged[slot_source], nothing)  11.3 us
    dot_general x1, matrix products, body(): jnp.einsum('nlw,nly->nwy', flattened_up, flattened_down, preferred_elemen...  8.23 us
    select_n x2, other arithmetic, body(): outgoing = jnp.where(active_slot_mask, merged[slot_source], nothing)  6.46 us
  transfers between devices with their start and end apart: 1, of which 1 were waited for; matrix products, arithmetic and copies ran while one was open for 1% of the time, Pallas kernels for 0%

commit v1 on v0

v1 whole, which is shorter than its diff:
```python
import jax
import jax.numpy as jnp
from jax import lax
from jax.experimental import pallas as pl
from jax.experimental.pallas import tpu as pltpu
from jax.sharding import PartitionSpec as P

CAP = 8
STEP = 8
scaling = 0.125
VMEM = 40 * 1024 * 1024


def slot_tables(file_sizes, file_writer, tensors):
    writers = jnp.arange(file_writer.shape[0], dtype=jnp.int32)
    starts = jnp.cumsum(file_sizes) - file_sizes
    number = jnp.arange(tensors, dtype=jnp.int32)[:, None]
    inside = (number >= starts[None, :]) & (number < (starts + file_sizes)[None, :])
    place = jnp.sum(jnp.where(inside, file_writer[None, :] * CAP + number - starts[None, :], 0), axis=1)
    size_of = jnp.sum(jnp.where(file_writer[None, :] == writers[:, None], file_sizes[None, :], 0), axis=1)
    return place.astype(jnp.int32), size_of.astype(jnp.int32)


def merge_kernel(place_ref, base_ref, up_ref, down_ref, out_ref, held, sems):
    step = pl.program_id(0)
    steps = pl.num_programs(0)
    slot = lax.rem(step, 2)

    def copy(slot, at, i):
        return pltpu.make_async_copy(held.at[slot, i], out_ref.at[place_ref[at * STEP + i]], sems.at[slot, i])

    @pl.when(step >= 2)
    def _():
        for i in range(STEP):
            copy(slot, step - 2, i).wait()

    for i in range(STEP):
        delta = lax.dot_general(
            up_ref[i], down_ref[i], (((0,), (0,)), ((), ())), preferred_element_type=jnp.float32
        )
        held[slot, i] = (base_ref[i].astype(jnp.float32) + scaling * delta).astype(jnp.bfloat16)
        copy(slot, step, i).start()

    @pl.when(step == steps - 1)
    def _():
        for i in range(STEP):
            copy(1 - slot, step - 1, i).wait()
        for i in range(STEP):
            copy(slot, step, i).wait()


def merge(place, base, up, down, slots):
    tensors, rows, cols = base.shape
    rank = up.shape[1]
    return pl.pallas_call(
        merge_kernel,
        out_shape=jax.ShapeDtypeStruct((slots, rows, cols), jnp.bfloat16),
        grid_spec=pltpu.PrefetchScalarGridSpec(
            num_scalar_prefetch=1,
            grid=(tensors // STEP,),
            in_specs=[
                pl.BlockSpec((STEP, rows, cols), lambda s, p: (s, 0, 0)),
                pl.BlockSpec((STEP, rank, rows), lambda s, p: (s, 0, 0)),
                pl.BlockSpec((STEP, rank, cols), lambda s, p: (s, 0, 0)),
            ],
            out_specs=pl.BlockSpec(memory_space=pl.ANY),
            scratch_shapes=[
                pltpu.VMEM((2, STEP, rows, cols), jnp.bfloat16),
                pltpu.SemaphoreType.DMA((2, STEP)),
            ],
        ),
        compiler_params=pltpu.CompilerParams(vmem_limit_bytes=VMEM),
        name="merge",
    )(place, base, up, down)


def unpack_kernel(count_ref, arrived_ref, out_ref):
    slot = pl.program_id(0)
    sources, _, _, cols = arrived_ref.shape

    @pl.when(slot < count_ref[0])
    def _():
        for e in range(sources):
            out_ref[0, :, e * cols : (e + 1) * cols] = arrived_ref[e, 0]

    @pl.when(slot >= count_ref[0])
    def _():
        out_ref[...] = jnp.zeros_like(out_ref)


def unpack(count, arrived):
    sources, slots, rows, cols = arrived.shape
    return pl.pallas_call(
        unpack_kernel,
        out_shape=jax.ShapeDtypeStruct((slots, rows, sources * cols), jnp.bfloat16),
        grid_spec=pltpu.PrefetchScalarGridSpec(
            num_scalar_prefetch=1,
            grid=(slots,),
            in_specs=[pl.BlockSpec((sources, 1, rows, cols), lambda s, n: (0, s, 0, 0))],
            out_specs=pl.BlockSpec((1, rows, sources * cols), lambda s, n: (s, 0, 0)),
        ),
        compiler_params=pltpu.CompilerParams(vmem_limit_bytes=VMEM),
        name="unpack",
    )(count, arrived)


def body(base_weights, adapter_up_factor, adapter_down, file_sizes, file_writer):
    writers = lax.axis_size("expert")
    tensors = base_weights.shape[0] * base_weights.shape[1]
    base = base_weights.reshape(tensors, *base_weights.shape[2:])
    up = adapter_up_factor.reshape(tensors, *adapter_up_factor.shape[2:])
    down_here = adapter_down.reshape(tensors, *adapter_down.shape[2:])
    place, size_of = slot_tables(file_sizes, file_writer, tensors)
    down = lax.all_gather(down_here, "row", axis=1, tiled=True)
    outgoing = merge(place, base, up, down, writers * CAP)
    outgoing = outgoing.reshape(writers, CAP, *outgoing.shape[1:])
    arrived = lax.all_to_all(outgoing, "expert", split_axis=0, concat_axis=0)
    count = lax.dynamic_slice(size_of, (lax.axis_index("expert"),), (1,))
    return unpack(count, arrived)


def solution(mesh):
    in_specs = (
        P(None, None, "row", "expert"),
        P(None, None, None, "row"),
        P(None, None, "row", "expert"),
        P(),
        P(),
    )
    out_specs = P("expert", "row", None)
    return jax.shard_map(body, mesh=mesh, in_specs=in_specs, out_specs=out_specs, check_vma=False)
```

time: 264 us -> 266 us (level)
  waiting for transfers between devices: 29.7 us -> 218 us
  blocking collectives: 148 us -> 0 us
  local copies, waits for them, and re-layouts: 55.7 us -> 7.33 us
  Pallas kernels: 0 us -> 17.8 us
  matrix products: 8.23 us -> 0 us
  starting transfers between devices: 0.01 us -> 7 us
  other arithmetic: 8.14 us -> 1.68 us
    all_to_all x0 -> x1, waiting for transfers between devices: none -> 188 us  [body(): arrived = lax.all_to_all(outgoing, 'expert', split_axis=0, concat_axis=0)]
    all_to_all x1 -> x0, blocking collectives: 148 us -> none  [body(): lax.all_to_all(outgoing, 'expert', split_axis=0, concat_axis=3, tiled=True)]
    all_to_all x1 -> x0, local copies, waits for them, and re-layouts: 24.1 us -> none  [body(): lax.all_to_all(outgoing, 'expert', split_axis=0, concat_axis=3, tiled=True)]
    squeeze x1 -> x0, local copies, waits for them, and re-layouts: 19.5 us -> none  [body(): return arrived[0]]
    pallas_call x0 -> x2, Pallas kernels: none -> 17.8 us  [the longest x1 12.2 us: unpack(): pl.pallas_call(unpack_kernel, out_shape=jax.ShapeDtypeStruct((slots, rows...]
    gather x1 -> x0, local copies, waits for them, and re-layouts: 11.3 us -> none  [body(): outgoing = jnp.where(active_slot_mask, merged[slot_source], nothing)]
    dot_general x1 -> x0, matrix products: 8.23 us -> none  [body(): jnp.einsum('nlw,nly->nwy', flattened_up, flattened_down, preferred_elemen...]
    all_to_all x0 -> x1, starting transfers between devices: none -> 6.99 us  [body(): arrived = lax.all_to_all(outgoing, 'expert', split_axis=0, concat_axis=0)]
  transfers between devices with their start and end apart: 1 -> 2, of which waited for: 1 -> 2; matrix products, arithmetic and copies ran while one was open for 1% -> 1% of each run, Pallas kernels for 0% -> 0%
where the time goes in v1:
time: 266 us; the launch traced here: 265 us
  waiting for transfers between devices  218 us (82%)
  Pallas kernels  17.8 us (7%)
  between operations  13.4 us (5%)
  local copies, waits for them, and re-layouts  7.33 us (3%)
  starting transfers between devices  7 us (3%)
    all_to_all x1, waiting for transfers between devices, body(): arrived = lax.all_to_all(outgoing, 'expert', split_axis=0, concat_axis=0)  188 us
    all_gather x1, waiting for transfers between devices, body(): down = lax.all_gather(down_here, 'row', axis=1, tiled=True)  29.2 us
    pallas_call x1, Pallas kernels, unpack(): pl.pallas_call(unpack_kernel, out_shape=jax.ShapeDtypeStruct((slots, rows...  12.2 us
    all_to_all x1, starting transfers between devices, body(): arrived = lax.all_to_all(outgoing, 'expert', split_axis=0, concat_axis=0)  6.99 us
    unnamed x10, local copies, waits for them, and re-layouts  5.98 us
    pallas_call x1, Pallas kernels, merge(): pl.pallas_call(merge_kernel, out_shape=jax.ShapeDtypeStruct((slots, rows,...  5.57 us
  transfers between devices with their start and end apart: 2, of which 2 were waited for; matrix products, arithmetic and copies ran while one was open for 1% of the time, Pallas kernels for 0%

profile of v1, /device:TPU:0, one launch (start us, length us, event | category | flops | bytes accessed | tf_op | source)
XLA Modules:
  0.0 265.2 jit_solution(5367268174959101323)
XLA Ops:
  6.5 0.0 all-gather.2.cloned.1.call-start
  6.5 0.7 all-gather.2.cloned.1.call-update
  7.3 0.7 copy.8
  8.0 0.1 reduce
  8.1 0.7 sub.4
  8.8 0.7 broadcast_multiply_fusion
  9.5 0.1 select_reduce_fusion.place_ref
  9.6 29.2 %all-gather.2.cloned.1.call-done.down_ref = bf16[64,64,256]{2,1,0:T(8,128)(2,1)} async-done(((bf16[64,8,256]{2,1,0:T(8,128)(2,1)}), bf16[64,64,256]{2,1,0:T(8,128)(2,1)}) %all-gather.2.cloned.1.call-update) | async-done | bytes 2097168 | tf_op jit(solution)/shard_map/all_gather | solution.py:114
  38.8 0.0 copy-start
  38.8 2.8 %copy-done = bf16[32,2,192,256]{3,2,1,0:T(8,128)(2,1)S(1)} copy-done((bf16[32,2,192,256]{3,2,1,0:T(8,128)(2,1)S(1)}, bf16[32,2,192,256]{3,2,1,0:T(8,128)(2,1)}, u32[]{:S(2)}) %copy-start) | copy-done | bytes 6291480
  41.6 0.0 copy-start.1
  41.6 1.6 copy-done.1
  43.2 0.0 copy-start.2
  43.2 1.6 copy-done.2
  44.8 5.6 %merge.1 = bf16[128,192,256]{2,1,0:T(8,128)(2,1)} custom-call(s32[64]{0:T(128)S(1)} %select_reduce_fusion.place_ref, bf16[64,192,256]{2,1,0:T(8,128)(2,1)S(1)} %bitcast.5, bf16[64,64,192]{2,1,0:T(8,128)(2,1)S(1)} %bitcast.6, bf16[64,64,256]{2,1,0:T(8,128)(2,1)S(1)} %copy-done.2), custom_call_target="tpu_custom_call" | custom-call | tf_op jit(solution)/shard_map/merge/pallas_call | solution.py:55
  50.4 0.0 copy-start.3
  50.4 0.0 copy-start.4
  50.4 7.0 %all-to-all-start = ((bf16[16,8,192,256]{3,2,1,0:T(8,128)(2,1)}), bf16[16,8,192,256]{3,2,1,0:T(8,128)(2,1)}, u32[]{:S(2)}, u32[]{:S(2)}) async-start(bf16[16,8,192,256]{3,2,1,0:T(8,128)(2,1)} %bitcast.7), calls=%async_computation | async-start | bytes 25165824 | tf_op jit(solution)/shard_map/all_to_all | solution.py:117
  57.4 0.0 copy-done.3
  57.4 0.0 copy-done.4
  57.4 0.1 select_reduce_fusion.1
  57.5 0.6 dynamic_slice.3.count_ref
  58.1 188.1 %all-to-all-done.arrived_ref = bf16[16,8,192,256]{3,2,1,0:T(8,128)(2,1)} async-done(((bf16[16,8,192,256]{3,2,1,0:T(8,128)(2,1)}), bf16[16,8,192,256]{3,2,1,0:T(8,128)(2,1)}, u32[]{:S(2)}, u32[]{:S(2)}) %all-to-all-start) | async-done | bytes 12582944 | tf_op jit(solution)/shard_map/all_to_all | solution.py:117
  246.2 12.2 %unpack.1 = bf16[8,192,4096]{2,1,0:T(8,128)(2,1)} custom-call(s32[1]{0:T(128)} %dynamic_slice.3.count_ref, bf16[16,8,192,256]{3,2,1,0:T(8,128)(2,1)} %all-to-all-done.arrived_ref), custom_call_target="tpu_custom_call" | custom-call | tf_op jit(solution)/shard_map/unpack/pallas_call | solution.py:93
  (1 shorter events, 0.0 us)
Async XLA Ops:
  6.5 32.3 %all-gather.2.cloned.1.call-start = ((), (), s32[]{:S(2)}) async-start(), calls=%async_computation.1 | async-start | bytes 2359296 | tf_op jit(solution)/shard_map/all_gather | solution.py:114
  38.8 2.8 %copy-start = (bf16[32,2,192,256]{3,2,1,0:T(8,128)(2,1)S(1)}, bf16[32,2,192,256]{3,2,1,0:T(8,128)(2,1)}, u32[]{:S(2)}) copy-start(bf16[32,2,192,256]{3,2,1,0:T(8,128)(2,1)} %param.5) | copy-start | bytes 18874372
  41.6 1.6 copy-start.1
  43.2 1.6 copy-start.2
  50.4 7.0 %copy-start.3 = (s32[16]{0:T(128)S(1)}, s32[16]{0:T(128)}, u32[]{:S(2)}) copy-start(s32[16]{0:T(128)} %param.8) | copy-start | bytes 196
  50.4 7.0 %copy-start.4 = (s32[16]{0:T(128)S(1)}, s32[16]{0:T(128)}, u32[]{:S(2)}) copy-start(s32[16]{0:T(128)} %param.9) | copy-start | bytes 196
  50.4 195.8 %all-to-all-start = ((bf16[16,8,192,256]{3,2,1,0:T(8,128)(2,1)}), bf16[16,8,192,256]{3,2,1,0:T(8,128)(2,1)}, u32[]{:S(2)}, u32[]{:S(2)}) async-start(bf16[16,8,192,256]{3,2,1,0:T(8,128)(2,1)} %bitcast.7), calls=%async_computation | async-start | bytes 25165824 | tf_op jit(solution)/shard_map/all_to_all | solution.py:117
Sparse Core Ops, SparseCore 0:
  9.0 29.7 all-gather.1
